TPU v7x, 128 devices: a whole 4x4x4 slice. The times are simulated.
128 devices in a mesh: head: 4 (over x), outer: 8 (over y_hi, z), inner: 4 (over y_lo, core).
Axes of the slice: x: 4, y: 4 (y_hi: 2, y_lo: 2; y = y_hi * 2 + y_lo), z: 4, core: 2. Of those that a mesh axis runs over, the one named last changes fastest.
Arguments:
- queries: bfloat16 [8192, 8192], P(('outer', 'inner'), 'head')
- keys: bfloat16 [8192, 1024], P(('outer', 'inner'), 'head')
- values: bfloat16 [8192, 1024], P(('outer', 'inner'), 'head'), may hold values from -6 to 6
- positions: int32 [8192], P(('outer', 'inner')), may hold values from 0 to 8191, as said below
- residual: float32 [32, 256, 8192], P(('outer', 'inner'), 'head'), may hold values from -1.2 to 1.2
- gain: float32 [8192], replicated, may hold values from 0.1 to 1.9
Outputs:
- stream: float32 [32, 256, 8192], P(('outer', 'inner'), 'head')
- normed: bfloat16 [32, 256, 8192], P(('outer', 'inner'), 'head')
Inputs may be any that keep to these rules, and one draw needn't show every extreme that they name: positions holds each of 0 to 8191 once; each aligned run of 128 rows holds consecutive positions in increasing order.
All inputs are finite; a program needn't handle non-finite values.
Results may differ from a plain program's by a relative error of at most 0.0075.
Values may be sent and summed in bfloat16 or wider, within the bound.
A program may use at most 128 MiB of HBM per device.

v0:
```python
import jax
import jax.numpy as jnp
from jax import lax
from jax.experimental import pallas as pl
from jax.experimental.pallas import tpu as pltpu
from jax.sharding import PartitionSpec as P

HD = 128
ROWS = 256
GROUP = 8
PART = 32
TILES = 16
TILE = GROUP * PART
MSG = 2 * ROWS + 32
CHUNK = 4 * ROWS
STEPS = 8
EARLY = 5
HIDDEN = -1e30
MESH = pl.DeviceIdType.MESH

PLACES = [(0, 0), (1, 0), (3, 0), (0, 1), (0, 3), (2, 0), (0, 2),
          (1, 1), (3, 3), (1, 3), (3, 1), (2, 1), (2, 3), (1, 2), (3, 2), (2, 2)]


def dot(a, b):
    return jnp.dot(a, b, preferred_element_type=jnp.float32)


def dot_nt(a, b):
    return lax.dot_general(a, b, (((1,), (1,)), ((), ())), preferred_element_type=jnp.float32)


def forwards(place):
    out = []
    if place == 0:
        for j, (dz, dy) in enumerate(PLACES[1:7], 1):
            out += [(0, dz, dy, j), (1, dz, dy, j)]
        return out
    dz, dy = PLACES[place]
    for step in (1, 3, 2):
        if dy == 0:
            out.append((0, 0, step, PLACES.index((dz, step))))
        elif dz == 0:
            out.append((1, step, 0, PLACES.index((step, dy))))
    return out


SENDS = [(j,) + f for j in range(16) for f in forwards(j)]


def kernel(
    pos_ref, q_hbm, k_hbm, v_hbm, res_hbm, gain_ref, stream_hbm, normed_hbm,
    kv, other, bias, qraw, qx, top, acc, obuf, att, res, sbuf, nbuf,
    stage_sem, kv_send, kv_recv, q_send, q_recv, sib_send, att_send, att_recv, res_sem, out_sem,
):
    x = lax.axis_index("head")
    outer = lax.axis_index("outer")
    inner = lax.axis_index("inner")
    y_hi, z = outer // 4, lax.rem(outer, 4)
    y_lo, c = inner // 2, lax.rem(inner, 2)
    y = y_hi * 2 + y_lo
    sib = 1 - c

    def chip(dx, dz, dy, core):
        zz, yy = lax.rem(z + dz, 4), lax.rem(y + dy, 4)
        return (lax.rem(x + dx, 4), (yy // 2) * 4 + zz, lax.rem(yy, 2) * 2 + core)

    mine = pl.ds(pl.multiple_of(c * HD, HD), HD)
    theirs = pl.ds(pl.multiple_of(sib * HD, HD), HD)
    stage = [
        pltpu.make_async_copy(k_hbm.at[:, mine], kv.at[c, pl.ds(0, ROWS)], stage_sem.at[0]),
        pltpu.make_async_copy(v_hbm.at[:, mine], kv.at[c, pl.ds(ROWS, ROWS)], stage_sem.at[1]),
        pltpu.make_async_copy(k_hbm.at[:, theirs], other.at[pl.ds(0, ROWS)], stage_sem.at[2]),
        pltpu.make_async_copy(v_hbm.at[:, theirs], other.at[pl.ds(ROWS, ROWS)], stage_sem.at[3]),
    ]
    for copy in stage:
        copy.start()
    wide = GROUP * HD
    q_mine = pltpu.make_async_copy(
        q_hbm.at[:, pl.ds(pl.multiple_of(c * wide, wide), wide)], qraw.at[c], stage_sem.at[4]
    )
    q_mine.start()
    res_in = pltpu.make_async_copy(res_hbm, res, res_sem)
    res_in.start()

    partners = [chip(0, 0, 0, sib)]
    partners += [chip(0, dz, dy, c) for dz, dy in PLACES[1:7]]
    partners += [chip(dx, 0, 0, core) for dx in (1, 2, 3) for core in (c, sib)]
    barrier = pltpu.get_barrier_semaphore()
    for partner in partners:
        pl.semaphore_signal(barrier, inc=1, device_id=partner, device_id_type=MESH)

    for run in range(2):
        block = (pos_ref[run : run + 1, :] >> 7).astype(jnp.float32)
        tile = jnp.broadcast_to(block, (16, HD)).astype(jnp.bfloat16)
        kv[c, 2 * ROWS + 16 * run : 2 * ROWS + 16 * run + 16, :] = tile
        other[2 * ROWS + 16 * run : 2 * ROWS + 16 * run + 16, :] = tile
    for copy in stage:
        copy.wait()
    pl.semaphore_wait(barrier, len(partners))

    def kv_copy(index):
        place, half, dz, dy, there = SENDS[index]
        return pltpu.make_async_remote_copy(
            src_ref=kv.at[2 * place + half],
            dst_ref=kv.at[2 * there + half],
            send_sem=kv_send.at[index],
            recv_sem=kv_recv.at[2 * there + half],
            device_id=chip(0, dz, dy, c),
            device_id_type=MESH,
        )

    def first_copy(n, half):
        dz, dy = PLACES[1 + n]
        return pltpu.make_async_remote_copy(
            src_ref=kv.at[half],
            dst_ref=kv.at[2 * (1 + n) + half],
            send_sem=kv_send.at[2 * n + half],
            recv_sem=kv_recv.at[2 * (1 + n) + half],
            device_id=chip(0, dz, dy, c),
            device_id_type=MESH,
        )

    def arrival(slot):
        return pltpu.make_async_remote_copy(
            src_ref=kv.at[slot],
            dst_ref=kv.at[slot],
            send_sem=kv_send.at[0],
            recv_sem=kv_recv.at[slot],
            device_id=chip(0, 0, 0, sib),
            device_id_type=MESH,
        )

    to_sib = pltpu.make_async_remote_copy(
        src_ref=other, dst_ref=kv.at[c], send_sem=sib_send, recv_sem=kv_recv.at[c],
        device_id=chip(0, 0, 0, sib), device_id_type=MESH,
    )
    to_sib.start()
    q_out = pltpu.make_async_remote_copy(
        src_ref=q_hbm.at[:, pl.ds(pl.multiple_of(sib * wide, wide), wide)],
        dst_ref=qraw.at[c],
        send_sem=q_send,
        recv_sem=q_recv,
        device_id=chip(0, 0, 0, sib),
        device_id_type=MESH,
    )
    q_out.start()
    for n in range(4):
        first_copy(n, c).start()
    arrival(sib).wait_recv()
    for n in range(4):
        first_copy(n, sib).start()
    for n in (4, 5):
        first_copy(n, c).start()
        first_copy(n, sib).start()

    lane = lax.broadcasted_iota(jnp.int32, (16, HD), 1)
    own = jnp.zeros((16, HD), jnp.float32)
    for run in range(4):
        at = 2 * ROWS + 16 * (run % 2)
        own = jnp.where(lane == run, kv[run // 2, at : at + 16, :].astype(jnp.float32), own)

    def fill_bias(slot):
        for run in range(2):
            block = kv[slot, 2 * ROWS + 16 * run : 2 * ROWS + 16 * run + 16, :].astype(jnp.float32)
            tile = jnp.where(block < own, 0.0, HIDDEN).astype(jnp.bfloat16)
            for r in range(8):
                bias[slot, run * HD + 16 * r : run * HD + 16 * r + 16, :] = tile

    q_mine.wait()
    q_in = pltpu.make_async_remote_copy(
        src_ref=qraw.at[sib], dst_ref=qraw.at[sib], send_sem=q_send, recv_sem=q_recv,
        device_id=chip(0, 0, 0, sib), device_id_type=MESH,
    )
    q_in.wait_recv()
    scale = 1.4426950408889634 / HD**0.5
    lanes = lax.broadcasted_iota(jnp.int32, (TILE, HD), 1)
    row = lax.rem(lax.broadcasted_iota(jnp.int32, (TILE, HD), 0), PART)

    def begin(tile, carry):
        shard, part = tile // 8, lax.rem(tile, 8)
        run = part // 4
        rows = pl.ds(pl.multiple_of(part * PART, PART), PART)
        for h in range(GROUP):
            piece = qraw[shard, rows, h * HD : (h + 1) * HD].astype(jnp.float32) * scale
            qx[tile, h * PART : (h + 1) * PART, :HD] = piece.astype(jnp.bfloat16)
        qx[tile, :, HD:] = jnp.where(lanes == 2 * shard + run, 1.0, 0.0).astype(jnp.bfloat16)
        keys = pl.ds(pl.multiple_of(run * HD, HD), HD)
        vals = pl.ds(pl.multiple_of(ROWS + run * HD, HD), HD)
        s = dot_nt(qx[tile, :, :HD], kv[shard, keys, :])
        s = jnp.where(lanes <= row + lax.rem(part, 4) * PART, s, HIDDEN)
        high = jnp.broadcast_to(jnp.max(s, axis=1, keepdims=True), (TILE, HD))
        p = jnp.exp2(s - high).astype(jnp.bfloat16)
        v = kv[shard, vals, :]
        top[tile] = high
        acc[tile] = dot(p, jnp.concatenate([v, jnp.ones_like(v)], axis=1))
        return carry

    lax.fori_loop(0, TILES, begin, 0, unroll=4)

    def attend(tile, step):
        k = jnp.concatenate([kv[4 * step + a, :ROWS, :] for a in range(4)], axis=0)
        b = jnp.concatenate([bias[4 * step + a] for a in range(4)], axis=0)
        v = jnp.concatenate([kv[4 * step + a, ROWS : 2 * ROWS, :] for a in range(4)], axis=0)
        s = dot_nt(qx[tile], jnp.concatenate([k, b], axis=1))
        before = top[tile]
        high = jnp.maximum(before, jnp.max(s, axis=1, keepdims=True))
        p = jnp.exp2(s - high[:, :1]).astype(jnp.bfloat16)
        fade = jnp.exp2(before - high)
        top[tile] = high
        acc[tile] = acc[tile] * jnp.concatenate([fade, fade], axis=1) + dot(
            p, jnp.concatenate([v, jnp.ones_like(v)], axis=1)
        )

    def receive(step):
        for i in range(STEPS):

            @pl.when(step == i)
            def _():
                for place in (2 * i, 2 * i + 1):
                    if place:
                        for half in range(2):
                            arrival(2 * place + half).wait_recv()
                    for index, send in enumerate(SENDS):
                        if send[0] == place and place:
                            kv_copy(index).start()

        for a in range(4):
            fill_bias(4 * step + a)

    def early(step, carry):
        receive(step)
        for tile in range(TILES):
            attend(tile, step)
        return carry

    lax.fori_loop(0, EARLY, early, 0)

    def rest(step, carry):
        receive(step)
        return carry

    lax.fori_loop(EARLY, STEPS, rest, 0)

    def att_copy(g, dx):
        half, shard = g // 2, lax.rem(c + 1 + g, 2)
        there = lax.rem(x + dx, 4)
        tile = shard * 8 + there * 2 + half
        return tile, pltpu.make_async_remote_copy(
            src_ref=obuf.at[tile],
            dst_ref=att.at[half, 2 * x + c],
            send_sem=att_send.at[tile],
            recv_sem=att_recv.at[half, 2 * x + c],
            device_id=chip(dx, 0, 0, shard),
            device_id_type=MESH,
        )

    def finish(g, carry):
        half, shard = g // 2, lax.rem(c + 1 + g, 2)
        for step in range(EARLY, STEPS):
            for quarter in range(4):
                attend(shard * 8 + quarter * 2 + half, step)
        for quarter in range(4):
            tile = shard * 8 + quarter * 2 + half
            both = acc[tile]
            o = (both[:, :HD] / both[:, HD:]).astype(jnp.bfloat16)
            for h in range(GROUP):
                obuf[tile, :, h * HD : (h + 1) * HD] = o[h * PART : (h + 1) * PART, :]
        for dx in (1, 2, 3):
            att_copy(g, dx)[1].start()

        @pl.when(lax.rem(g, 2) == 0)
        def _():
            att_copy(g, 0)[1].start()

        @pl.when(lax.rem(g, 2) == 1)
        def _():
            att[half, 2 * x + c] = obuf[c * 8 + x * 2 + half]

        return carry

    lax.fori_loop(0, 4, finish, 0)

    def finalize(half):
        for n in range(1, 8):
            source = lax.rem(2 * x + c + n, 8)
            pltpu.make_async_remote_copy(
                src_ref=att.at[half, source], dst_ref=att.at[half, source], send_sem=q_send,
                recv_sem=att_recv.at[half, source], device_id=chip(0, 0, 0, sib), device_id_type=MESH,
            ).wait_recv()

        def rows16(i, carry):
            rows = pl.ds(pl.multiple_of(half * PART + 16 * i, 16), 16)
            local = pl.ds(pl.multiple_of(16 * i, 16), 16)
            squares = jnp.zeros((16, HD), jnp.float32)
            for source in range(8):
                cols = slice(source * wide, (source + 1) * wide)
                s = res[rows, cols] + att[half, source, local, :].astype(jnp.float32)
                sbuf[rows, cols] = s
                sq = s * s
                for a in range(8):
                    squares += sq[:, a * HD : (a + 1) * HD]
            inv = lax.rsqrt(jnp.sum(squares, axis=1, keepdims=True) * (1.0 / (8 * wide)) + 1e-05)
            for source in range(8):
                cols = slice(source * wide, (source + 1) * wide)
                nbuf[rows, cols] = (sbuf[rows, cols] * inv * gain_ref[:, cols]).astype(jnp.bfloat16)
            return carry

        lax.fori_loop(0, 2, rows16, 0)
        rows = pl.ds(half * PART, PART)
        outs = [
            pltpu.make_async_copy(sbuf.at[rows], stream_hbm.at[rows], out_sem.at[2 * half]),
            pltpu.make_async_copy(nbuf.at[rows], normed_hbm.at[rows], out_sem.at[2 * half + 1]),
        ]
        for copy in outs:
            copy.start()
        return outs

    res_in.wait()
    outs = finalize(0) + finalize(1)
    to_sib.wait_send()
    q_out.wait_send()
    for n in range(6):
        for half in range(2):
            first_copy(n, half).wait_send()
    for index in range(12, len(SENDS)):
        kv_copy(index).wait_send()

    def sent(g, carry):
        for dx in (1, 2, 3):
            att_copy(g, dx)[1].wait_send()

        @pl.when(lax.rem(g, 2) == 0)
        def _():
            att_copy(g, 0)[1].wait_send()

        return carry

    lax.fori_loop(0, 4, sent, 0)
    for copy in outs:
        copy.wait()


def per_device(queries, keys, values, positions, residual, gain):
    width = residual.shape[2]
    rows = residual.shape[1]
    hbm = pl.BlockSpec(memory_space=pl.ANY)
    vmem = pl.BlockSpec(memory_space=pltpu.VMEM)
    dma = pltpu.SemaphoreType.DMA
    bf16, f32 = jnp.bfloat16, jnp.float32
    stream, normed = pl.pallas_call(
        kernel,
        out_shape=(
            jax.ShapeDtypeStruct((rows, width), f32),
            jax.ShapeDtypeStruct((rows, width), bf16),
        ),
        in_specs=[vmem, hbm, hbm, hbm, hbm, vmem],
        out_specs=(hbm, hbm),
        scratch_shapes=[
            pltpu.VMEM((32, MSG, HD), bf16),
            pltpu.VMEM((MSG, HD), bf16),
            pltpu.VMEM((32, ROWS, HD), bf16),
            pltpu.VMEM((2, ROWS, GROUP * HD), bf16),
            pltpu.VMEM((TILES, TILE, 2 * HD), bf16),
            pltpu.VMEM((TILES, TILE, HD), f32),
            pltpu.VMEM((TILES, TILE, 2 * HD), f32),
            pltpu.VMEM((TILES, PART, GROUP * HD), bf16),
            pltpu.VMEM((2, 8, PART, GROUP * HD), bf16),
            pltpu.VMEM((rows, width), f32),
            pltpu.VMEM((rows, width), f32),
            pltpu.VMEM((rows, width), bf16),
            dma((5,)),
            dma((len(SENDS),)),
            dma((32,)),
            dma,
            dma,
            dma,
            dma((TILES,)),
            dma((2, 8)),
            dma,
            dma((4,)),
        ],
        compiler_params=pltpu.CompilerParams(
            collective_id=0, has_side_effects=True, vmem_limit_bytes=60 * 2**20
        ),
    )(
        positions.reshape(2, HD), queries, keys, values, residual[0], gain.reshape(1, width)
    )
    return (stream[None], normed[None])


def solution(mesh):
    both = ("outer", "inner")
    return jax.shard_map(
        per_device,
        mesh=mesh,
        in_specs=(P(both, "head"), P(both, "head"), P(both, "head"), P(both), P(both, "head", None), P()),
        out_specs=(P(both, "head", None), P(both, "head", None)),
        check_vma=False,
    )
```

profile of v0, /device:TPU:0, one launch (start us, length us, event | category | flops | bytes accessed | tf_op | source)
XLA Modules:
  0.0 85.6 jit_solution(7215590589204945051)
XLA Ops:
  0.6 80.9 %shard_map.77 = (f32[64,8192]{1,0:T(8,128)}, bf16[64,8192]{1,0:T(8,128)(2,1)}) custom-call(s32[2,128]{1,0:T(2,128)} %bitcast.9, bf16[256,2048]{1,0:T(8,128)(2,1)} %q_hbm.1, bf16[256,256]{1,0:T(8,128)(2,1)} %k_hbm.1, bf16[256,256]{1,0:T(8,128)(2,1)} %v_hbm.1, f32[64,8192]{1,0:T(8,128)} %bitcast.5, f32[1,8192]{1,0:T(1,128)} %bitcast.8), custom_call_target="tpu_custom_call" | custom-call | tf_op jit(solution)/shard_map/pallas_call | solution.py:351
  81.5 0.0 copy-start
  81.5 3.1 %copy.10 = f32[1,64,8192]{2,1,0:T(8,128)} copy(f32[1,64,8192]{2,1,0:T(8,128)} %bitcast.6) | data formatting | bytes 4194304
  84.7 0.0 copy-done
  84.7 1.0 %copy.11 = bf16[1,64,8192]{2,1,0:T(8,128)(2,1)} copy(bf16[1,64,8192]{2,1,0:T(8,128)(2,1)S(1)} %bitcast.7) | data formatting | bytes 2097152
Async XLA Ops:
  81.5 3.2 %copy-start = (bf16[64,8192]{1,0:T(8,128)(2,1)S(1)}, bf16[64,8192]{1,0:T(8,128)(2,1)}, u32[]{:S(2)}) copy-start(bf16[64,8192]{1,0:T(8,128)(2,1)} %get-tuple-element.5) | copy-start | bytes 3145732
where the time goes:
time: 85.8 us; the launch traced here: 85.6 us
  Pallas kernels  80.9 us (94%)
  local copies, waits for them, and re-layouts  4.12 us (5%)
    pallas_call x1, Pallas kernels, per_device(): pl.pallas_call(kernel, out_shape=(jax.ShapeDtypeStruct((rows, width), f32...  80.9 us
    unnamed x4, local copies, waits for them, and re-layouts  4.12 us

commit v1 on v0

v1 whole, which is shorter than its diff:
```python
import jax
import jax.numpy as jnp
from jax import lax
from jax.experimental import pallas as pl
from jax.experimental.pallas import tpu as pltpu
from jax.sharding import PartitionSpec as P

HD = 128
ROWS = 256
GROUP = 8
PART = 32
TILES = 16
TILE = GROUP * PART
MSG = 2 * ROWS + 32
STEPS = 6
HIDDEN = -1e30
MESH = pl.DeviceIdType.MESH

PLACES = [(0, 0), (1, 0), (3, 0), (0, 1), (0, 3), (2, 0), (0, 2),
          (1, 1), (1, 3), (3, 1), (3, 3), (2, 1), (2, 3), (1, 2), (3, 2), (2, 2)]

SERVED = [(1, (1, 2, 3, 4), 1), (3, (5, 6, 7, 8), 0), (4, (9, 10), 0), (5, (5, 6, 7, 8), 1), (6, (9, 10), 1),
          (9, (11, 12, 13), 2), (10, (14,), 2)]
LAST = (13, 14, 15)
BAND = TILES // 2


def dot(a, b):
    return jnp.dot(a, b, preferred_element_type=jnp.float32)


def dot_nt(a, b):
    return lax.dot_general(a, b, (((1,), (1,)), ((), ())), preferred_element_type=jnp.float32)


def forwards(place):
    out = []
    here = PLACES[place]
    for half in range(2):
        a, b = here if half == 0 else here[::-1]
        there = []
        if a == 0 and b == 0:
            there += [(1, 0), (3, 0)]
        if a == 1 and b == 0:
            there.append((2, 0))
        if b == 0:
            there += [(a, 1), (a, 3)]
        if (b == 1 and a % 2 == 0) or (b == 3 and a % 2 == 1):
            there.append((a, 2))
        for na, nb in there:
            da, db = (na - a) % 4, (nb - b) % 4
            step, new = ((da, db), (na, nb)) if half == 0 else ((db, da), (nb, na))
            out.append((half,) + step + (PLACES.index(new),))
    return out


FIRST = forwards(0)
SENDS = [(j,) + f for j in range(16) for f in forwards(j)]
AROUND = [(1, 0), (3, 0), (0, 1), (0, 3)]


def kernel(
    pos_ref, q_hbm, k_hbm, v_hbm, att,
    kv, other, bias, qraw, qx, top, acc, obuf, s_even, s_odd, p_even, p_odd, f_even, f_odd,
    stage_sem, kv_send, kv_recv, q_send, q_recv, sib_send, att_send, att_recv, out_sem,
):
    x = lax.axis_index("head")
    outer = lax.axis_index("outer")
    inner = lax.axis_index("inner")
    y_hi, z = outer // 4, lax.rem(outer, 4)
    y_lo, c = inner // 2, lax.rem(inner, 2)
    y = y_hi * 2 + y_lo
    sib = 1 - c

    def chip(dx, dz, dy, core):
        zz, yy = lax.rem(z + dz, 4), lax.rem(y + dy, 4)
        return (lax.rem(x + dx, 4), (yy // 2) * 4 + zz, lax.rem(yy, 2) * 2 + core)

    mine = pl.ds(pl.multiple_of(c * HD, HD), HD)
    theirs = pl.ds(pl.multiple_of(sib * HD, HD), HD)
    stage = [
        pltpu.make_async_copy(k_hbm.at[:, mine], kv.at[c, pl.ds(0, ROWS)], stage_sem.at[0]),
        pltpu.make_async_copy(v_hbm.at[:, mine], kv.at[c, pl.ds(ROWS, ROWS)], stage_sem.at[1]),
        pltpu.make_async_copy(k_hbm.at[:, theirs], other.at[pl.ds(0, ROWS)], stage_sem.at[2]),
        pltpu.make_async_copy(v_hbm.at[:, theirs], other.at[pl.ds(ROWS, ROWS)], stage_sem.at[3]),
    ]
    for copy in stage:
        copy.start()
    wide = GROUP * HD
    q_mine = pltpu.make_async_copy(
        q_hbm.at[:, pl.ds(pl.multiple_of(c * wide, wide), wide)], qraw.at[c], stage_sem.at[4]
    )
    q_mine.start()

    partners = [chip(0, 0, 0, sib)]
    partners += [chip(0, dz, dy, c) for dz, dy in AROUND]
    partners += [chip(dx, 0, 0, core) for dx in (1, 2, 3) for core in (c, sib)]
    barrier = pltpu.get_barrier_semaphore()
    for partner in partners:
        pl.semaphore_signal(barrier, inc=1, device_id=partner, device_id_type=MESH)

    for run in range(2):
        block = (pos_ref[run : run + 1, :] >> 7).astype(jnp.float32)
        tile = jnp.broadcast_to(block, (16, HD)).astype(jnp.bfloat16)
        kv[c, 2 * ROWS + 16 * run : 2 * ROWS + 16 * run + 16, :] = tile
        other[2 * ROWS + 16 * run : 2 * ROWS + 16 * run + 16, :] = tile
    for copy in stage:
        copy.wait()
    pl.semaphore_wait(barrier, len(partners))

    def kv_copy(index):
        place, half, dz, dy, there = SENDS[index]
        return pltpu.make_async_remote_copy(
            src_ref=kv.at[2 * place + half],
            dst_ref=kv.at[2 * there + half],
            send_sem=kv_send.at[index],
            recv_sem=kv_recv.at[2 * there + half],
            device_id=chip(0, dz, dy, c),
            device_id_type=MESH,
        )

    def first_copy(n, half):
        dz, dy = AROUND[n]
        return pltpu.make_async_remote_copy(
            src_ref=kv.at[half],
            dst_ref=kv.at[2 * (1 + n) + half],
            send_sem=kv_send.at[2 * n + half],
            recv_sem=kv_recv.at[2 * (1 + n) + half],
            device_id=chip(0, dz, dy, c),
            device_id_type=MESH,
        )

    def arrival(slot):
        return pltpu.make_async_remote_copy(
            src_ref=kv.at[slot],
            dst_ref=kv.at[slot],
            send_sem=kv_send.at[0],
            recv_sem=kv_recv.at[slot],
            device_id=chip(0, 0, 0, sib),
            device_id_type=MESH,
        )

    to_sib = pltpu.make_async_remote_copy(
        src_ref=other, dst_ref=kv.at[c], send_sem=sib_send, recv_sem=kv_recv.at[c],
        device_id=chip(0, 0, 0, sib), device_id_type=MESH,
    )
    to_sib.start()
    q_out = pltpu.make_async_remote_copy(
        src_ref=q_hbm.at[:, pl.ds(pl.multiple_of(sib * wide, wide), wide)],
        dst_ref=qraw.at[c],
        send_sem=q_send,
        recv_sem=q_recv,
        device_id=chip(0, 0, 0, sib),
        device_id_type=MESH,
    )
    q_out.start()
    for n in range(4):
        first_copy(n, c).start()
    arrival(sib).wait_recv()
    for n in range(4):
        first_copy(n, sib).start()

    lane = lax.broadcasted_iota(jnp.int32, (16, HD), 1)
    own = jnp.zeros((16, HD), jnp.float32)
    for run in range(4):
        at = 2 * ROWS + 16 * (run % 2)
        own = jnp.where(lane == run, kv[run // 2, at : at + 16, :].astype(jnp.float32), own)

    def fill_bias(slot):
        for run in range(2):
            block = kv[slot, 2 * ROWS + 16 * run : 2 * ROWS + 16 * run + 16, :].astype(jnp.float32)
            tile = jnp.where(block < own, 0.0, HIDDEN).astype(jnp.bfloat16)
            for r in range(8):
                bias[slot, run * HD + 16 * r : run * HD + 16 * r + 16, :] = tile

    q_mine.wait()
    q_in = pltpu.make_async_remote_copy(
        src_ref=qraw.at[sib], dst_ref=qraw.at[sib], send_sem=q_send, recv_sem=q_recv,
        device_id=chip(0, 0, 0, sib), device_id_type=MESH,
    )
    q_in.wait_recv()
    scale = 1.4426950408889634 / HD**0.5
    lanes = lax.broadcasted_iota(jnp.int32, (TILE, HD), 1)
    row = lax.rem(lax.broadcasted_iota(jnp.int32, (TILE, HD), 0), PART)

    def begin(tile, carry):
        shard, part = tile // 8, lax.rem(tile, 8)
        run = part // 4
        rows = pl.ds(pl.multiple_of(part * PART, PART), PART)
        for h in range(GROUP):
            piece = qraw[shard, rows, h * HD : (h + 1) * HD].astype(jnp.float32) * scale
            qx[tile, h * PART : (h + 1) * PART, :HD] = piece.astype(jnp.bfloat16)
        qx[tile, :, HD:] = jnp.where(lanes == 2 * shard + run, 1.0, 0.0).astype(jnp.bfloat16)
        keys = pl.ds(pl.multiple_of(run * HD, HD), HD)
        vals = pl.ds(pl.multiple_of(ROWS + run * HD, HD), HD)
        diag = dot_nt(qx[tile, :, :HD], kv[shard, keys, :])
        diag = jnp.where(lanes <= row + lax.rem(part, 4) * PART, diag, HIDDEN)
        k, v = pair([0, 1])
        s = jnp.concatenate([diag, dot_nt(qx[tile], k)], axis=1)
        high = jnp.broadcast_to(jnp.max(s, axis=1, keepdims=True), (TILE, HD))
        p = jnp.exp2(s - high[:, :1]).astype(jnp.bfloat16)
        v = jnp.concatenate([kv[shard, vals, :], v], axis=0)
        top[tile] = high
        acc[tile] = dot(p, jnp.concatenate([v, jnp.ones_like(v)], axis=1))
        return carry

    def slots_of(places):
        return [2 * place + half for place in places for half in range(2)]

    def pair(slots):
        k = jnp.concatenate([kv[slot, :ROWS, :] for slot in slots], axis=0)
        b = jnp.concatenate([bias[slot] for slot in slots], axis=0)
        v = jnp.concatenate([kv[slot, ROWS : 2 * ROWS, :] for slot in slots], axis=0)
        return jnp.concatenate([k, b], axis=1), v

    for slot in range(2):
        fill_bias(slot)
    lax.fori_loop(0, TILES, begin, 0, unroll=4)

    scores, weights, fades = (s_even, s_odd), (p_even, p_odd), (f_even, f_odd)

    def score(tile, slots, b):
        k, _ = pair(slots)
        scores[b][:, : ROWS * len(slots)] = dot_nt(qx[tile], k)

    def weigh(tile, count, b):
        s = scores[b][:, : ROWS * count]
        before = top[tile]
        high = jnp.maximum(before, jnp.max(s, axis=1, keepdims=True))
        weights[b][:, : ROWS * count] = jnp.exp2(s - high[:, :1]).astype(jnp.bfloat16)
        fades[b][...] = jnp.exp2(before - high)
        top[tile] = high

    def gather(tile, slots, b):
        _, v = pair(slots)
        fade = fades[b][...]
        acc[tile] = acc[tile] * jnp.concatenate([fade, fade], axis=1) + dot(
            weights[b][:, : ROWS * len(slots)], jnp.concatenate([v, jnp.ones_like(v)], axis=1)
        )

    def serve(places, halves=(0, 1)):
        for place in places:
            for half in halves:
                arrival(2 * place + half).wait_recv()
                for index, send in enumerate(SENDS):
                    if send[:2] == (place, half):
                        kv_copy(index).start()
                fill_bias(2 * place + half)

    def slots_at(turn):
        step = turn // 2
        half = jnp.where(lax.rem(step, 2) == 0, c, sib)
        start = jnp.where(step < 4, 2 + 8 * (step // 2) + half, 4 * step + 2)
        stride = jnp.where(step < 4, 2, 1)
        return [start + stride * a for a in range(4)]

    def tile_at(turn, u):
        return lax.rem(turn, 2) * BAND + u

    for core in range(2):

        @pl.when(c == core)
        def _():
            serve((1, 2, 3, 4), (core,))

    score(0, slots_at(0), 0)

    def early(turn, carry):
        for i, places, which in SERVED:
            if which == 2:

                @pl.when(turn == i)
                def _():
                    serve(places)

            else:
                for core in range(2):

                    @pl.when((turn == i) & (c == core))
                    def _():
                        serve(places, ((core + which) % 2,))

        here = slots_at(turn)
        before = slots_at(jnp.maximum(turn - 1, 0))
        after = slots_at(jnp.minimum(turn + 1, 2 * STEPS - 1))
        for u in range(BAND):
            now, other_one = u % 2, (u + 1) % 2
            if u + 1 < BAND:
                score(tile_at(turn, u + 1), here, other_one)
            else:
                score(tile_at(turn + 1, 0), after, other_one)
            if u:
                gather(tile_at(turn, u - 1), here, other_one)
            else:
                gather(tile_at(turn + 1, BAND - 1), before, other_one)
            weigh(tile_at(turn, u), 4, now)
        return carry

    weights[1][...] = jnp.zeros_like(weights[1])
    fades[1][...] = jnp.ones_like(fades[1])
    lax.fori_loop(0, 2 * STEPS, early, 0)
    gather(TILES - 1, slots_at(2 * STEPS - 1), 1)
    serve((15,))

    def landing(half, source):
        cols = pl.ds(pl.multiple_of(source * wide, wide), wide)
        return att.at[pl.ds(pl.multiple_of(half * PART, PART), PART), cols]

    def own_copy(half):
        return pltpu.make_async_copy(
            obuf.at[c * 8 + x * 2 + half], landing(half, 2 * x + c), out_sem.at[half]
        )

    def att_copy(g, dx):
        half, shard = g // 2, lax.rem(c + 1 + g, 2)
        there = lax.rem(x + dx, 4)
        tile = shard * 8 + there * 2 + half
        return tile, pltpu.make_async_remote_copy(
            src_ref=obuf.at[tile],
            dst_ref=landing(half, 2 * x + c),
            send_sem=att_send.at[tile],
            recv_sem=att_recv.at[half, 2 * x + c],
            device_id=chip(dx, 0, 0, shard),
            device_id_type=MESH,
        )

    def finish(g, carry):
        half, shard = g // 2, lax.rem(c + 1 + g, 2)
        last = slots_of(LAST)
        tiles = [shard * 8 + quarter * 2 + half for quarter in range(4)]
        later = jnp.minimum(g + 1, 3)
        following = lax.rem(c + 1 + later, 2) * 8 + later // 2
        for u in range(4):
            score(tiles[u + 1] if u < 3 else following, last, (u + 1) % 2)
            if u:
                gather(tiles[u - 1], last, (u + 1) % 2)
            weigh(tiles[u], len(last), u % 2)
        gather(tiles[3], last, 1)
        for tile in tiles:
            both = acc[tile]
            o = (both[:, :HD] / both[:, HD:]).astype(jnp.bfloat16)
            for h in range(GROUP):
                obuf[tile, :, h * HD : (h + 1) * HD] = o[h * PART : (h + 1) * PART, :]
        for dx in (1, 2, 3):
            att_copy(g, dx)[1].start()

        @pl.when(lax.rem(g, 2) == 0)
        def _():
            att_copy(g, 0)[1].start()

        @pl.when(lax.rem(g, 2) == 1)
        def _():
            own_copy(half).start()

        return carry

    score(lax.rem(c + 1, 2) * 8, slots_of(LAST), 0)
    lax.fori_loop(0, 4, finish, 0)

    for half in range(2):
        for n in range(1, 8):
            source = lax.rem(2 * x + c + n, 8)
            pltpu.make_async_remote_copy(
                src_ref=landing(half, source), dst_ref=landing(half, source), send_sem=q_send,
                recv_sem=att_recv.at[half, source], device_id=chip(0, 0, 0, sib), device_id_type=MESH,
            ).wait_recv()
    to_sib.wait_send()
    q_out.wait_send()
    for n in range(4):
        for half in range(2):
            first_copy(n, half).wait_send()
    for index in range(len(FIRST), len(SENDS)):
        kv_copy(index).wait_send()

    def sent(g, carry):
        for dx in (1, 2, 3):
            att_copy(g, dx)[1].wait_send()

        @pl.when(lax.rem(g, 2) == 0)
        def _():
            att_copy(g, 0)[1].wait_send()

        return carry

    lax.fori_loop(0, 4, sent, 0)
    for half in range(2):
        own_copy(half).wait()


def update(att_ref, res_ref, gain_ref, stream_ref, normed_ref):
    stream = res_ref[...] + att_ref[...].astype(jnp.float32)
    stream_ref[...] = stream
    inv = lax.rsqrt(jnp.mean(stream * stream, axis=1, keepdims=True) + 1e-05)
    normed_ref[...] = (stream * inv * gain_ref[...]).astype(jnp.bfloat16)


def per_device(queries, keys, values, positions, residual, gain):
    width = residual.shape[2]
    rows = residual.shape[1]
    hbm = pl.BlockSpec(memory_space=pl.ANY)
    vmem = pl.BlockSpec(memory_space=pltpu.VMEM)
    dma = pltpu.SemaphoreType.DMA
    bf16, f32 = jnp.bfloat16, jnp.float32
    attended = pl.pallas_call(
        kernel,
        out_shape=jax.ShapeDtypeStruct((rows, width), bf16),
        in_specs=[vmem, hbm, hbm, hbm],
        out_specs=hbm,
        scratch_shapes=[
            pltpu.VMEM((32, MSG, HD), bf16),
            pltpu.VMEM((MSG, HD), bf16),
            pltpu.VMEM((32, ROWS, HD), bf16),
            pltpu.VMEM((2, ROWS, GROUP * HD), bf16),
            pltpu.VMEM((TILES, TILE, 2 * HD), bf16),
            pltpu.VMEM((TILES, TILE, HD), f32),
            pltpu.VMEM((TILES, TILE, 2 * HD), f32),
            pltpu.VMEM((TILES, PART, GROUP * HD), bf16),
            pltpu.VMEM((TILE, 6 * ROWS), f32),
            pltpu.VMEM((TILE, 6 * ROWS), f32),
            pltpu.VMEM((TILE, 6 * ROWS), bf16),
            pltpu.VMEM((TILE, 6 * ROWS), bf16),
            pltpu.VMEM((TILE, HD), f32),
            pltpu.VMEM((TILE, HD), f32),
            dma((5,)),
            dma((len(SENDS),)),
            dma((32,)),
            dma,
            dma,
            dma,
            dma((TILES,)),
            dma((2, 8)),
            dma((2,)),
        ],
        compiler_params=pltpu.CompilerParams(
            collective_id=0, has_side_effects=True, vmem_limit_bytes=60 * 2**20
        ),
    )(positions.reshape(2, HD), queries, keys, values)
    block = 16
    band = pl.BlockSpec((block, width), lambda i: (i, 0))
    stream, normed = pl.pallas_call(
        update,
        grid=(rows // block,),
        out_shape=(
            jax.ShapeDtypeStruct((rows, width), f32),
            jax.ShapeDtypeStruct((rows, width), bf16),
        ),
        in_specs=[band, band, pl.BlockSpec((1, width), lambda i: (0, 0))],
        out_specs=(band, band),
    )(attended, residual[0], gain.reshape(1, width))
    return (stream[None], normed[None])


def solution(mesh):
    both = ("outer", "inner")
    return jax.shard_map(
        per_device,
        mesh=mesh,
        in_specs=(P(both, "head"), P(both, "head"), P(both, "head"), P(both), P(both, "head", None), P()),
        out_specs=(P(both, "head", None), P(both, "head", None)),
        check_vma=False,
    )
```

time: 85.8 us -> 77.1 us (0.90); the launches traced: 85.6 us -> 76.1 us
  Pallas kernels: 80.9 us -> 75.4 us
  local copies, waits for them, and re-layouts: 4.12 us -> 0 us
    pallas_call x1 -> x2, Pallas kernels: 80.9 us -> 75.4 us  [the longest x1 71.1 us: per_device(): pl.pallas_call(kernel, out_shape=jax.ShapeDtypeStruct((rows, width), bf16...]
    unnamed x4 -> x0, local copies, waits for them, and re-layouts: 4.12 us -> none
where the time goes in v1:
time: 77.1 us; the launch traced here: 76.1 us
  Pallas kernels  75.4 us (98%)
    pallas_call x1, Pallas kernels, per_device(): pl.pallas_call(kernel, out_shape=jax.ShapeDtypeStruct((rows, width), bf16...  71.1 us
    pallas_call x1, Pallas kernels, per_device(): pl.pallas_call(update, grid=(rows // block,), out_shape=(jax.ShapeDtypeSt...  4.28 us

profile of v1, /device:TPU:0, one launch (start us, length us, event | category | flops | bytes accessed | tf_op | source)
XLA Modules:
  0.0 76.1 jit_solution(7914464816508610806)
XLA Ops:
  0.6 71.1 %shard_map.77.att_ref = bf16[64,8192]{1,0:T(8,128)(2,1)} custom-call(s32[2,128]{1,0:T(2,128)} %bitcast.7, bf16[256,2048]{1,0:T(8,128)(2,1)} %q_hbm.1, bf16[256,256]{1,0:T(8,128)(2,1)} %k_hbm.1, bf16[256,256]{1,0:T(8,128)(2,1)} %v_hbm.1), custom_call_target="tpu_custom_call" | custom-call | tf_op jit(solution)/shard_map/pallas_call | solution.py:404
  71.8 4.3 %shard_map.78 = (f32[64,8192]{1,0:T(8,128)}, bf16[64,8192]{1,0:T(8,128)(2,1)}) custom-call(bf16[64,8192]{1,0:T(8,128)(2,1)} %shard_map.77.att_ref, f32[64,8192]{1,0:T(8,128)} %bitcast.5, f32[1,8192]{1,0:T(1,128)} %bitcast.6), custom_call_target="tpu_custom_call" | custom-call | tf_op jit(solution)/shard_map/pallas_call | solution.py:440

commit v2 on v1

--- a/solution.py
+++ b/solution.py
@@ -12,7 +12,7 @@
 TILES = 16
 TILE = GROUP * PART
 MSG = 2 * ROWS + 32
-STEPS = 6
+STEPS = 5
 HIDDEN = -1e30
 MESH = pl.DeviceIdType.MESH
 
@@ -20,8 +20,9 @@
           (1, 1), (1, 3), (3, 1), (3, 3), (2, 1), (2, 3), (1, 2), (3, 2), (2, 2)]
 
 SERVED = [(1, (1, 2, 3, 4), 1), (3, (5, 6, 7, 8), 0), (4, (9, 10), 0), (5, (5, 6, 7, 8), 1), (6, (9, 10), 1),
-          (9, (11, 12, 13), 2), (10, (14,), 2)]
-LAST = (13, 14, 15)
+          (8, (11, 14), 2), (9, (12, 13), 2)]
+LATER = (9, 10)
+LAST = (11, 12, 13, 14, 15)
 BAND = TILES // 2
 
 
@@ -41,11 +42,11 @@
         there = []
         if a == 0 and b == 0:
             there += [(1, 0), (3, 0)]
-        if a == 1 and b == 0:
+        if a == (1, 3)[half] and b == 0:
             there.append((2, 0))
         if b == 0:
             there += [(a, 1), (a, 3)]
-        if (b == 1 and a % 2 == 0) or (b == 3 and a % 2 == 1):
+        if b == (1 if a in ((0, 2, 3), (3,))[half] else 3):
             there.append((a, 2))
         for na, nb in there:
             da, db = (na - a) % 4, (nb - b) % 4
@@ -185,23 +186,13 @@
 
     def begin(tile, carry):
         shard, part = tile // 8, lax.rem(tile, 8)
-        run = part // 4
         rows = pl.ds(pl.multiple_of(part * PART, PART), PART)
         for h in range(GROUP):
             piece = qraw[shard, rows, h * HD : (h + 1) * HD].astype(jnp.float32) * scale
             qx[tile, h * PART : (h + 1) * PART, :HD] = piece.astype(jnp.bfloat16)
-        qx[tile, :, HD:] = jnp.where(lanes == 2 * shard + run, 1.0, 0.0).astype(jnp.bfloat16)
-        keys = pl.ds(pl.multiple_of(run * HD, HD), HD)
-        vals = pl.ds(pl.multiple_of(ROWS + run * HD, HD), HD)
-        diag = dot_nt(qx[tile, :, :HD], kv[shard, keys, :])
-        diag = jnp.where(lanes <= row + lax.rem(part, 4) * PART, diag, HIDDEN)
-        k, v = pair([0, 1])
-        s = jnp.concatenate([diag, dot_nt(qx[tile], k)], axis=1)
-        high = jnp.broadcast_to(jnp.max(s, axis=1, keepdims=True), (TILE, HD))
-        p = jnp.exp2(s - high[:, :1]).astype(jnp.bfloat16)
-        v = jnp.concatenate([kv[shard, vals, :], v], axis=0)
-        top[tile] = high
-        acc[tile] = dot(p, jnp.concatenate([v, jnp.ones_like(v)], axis=1))
+        qx[tile, :, HD:] = jnp.where(lanes == 2 * shard + part // 4, 1.0, 0.0).astype(jnp.bfloat16)
+        top[tile] = jnp.full((TILE, HD), HIDDEN, jnp.float32)
+        acc[tile] = jnp.zeros((TILE, 2 * HD), jnp.float32)
         return carry
 
     def slots_of(places):
@@ -215,7 +206,7 @@
 
     for slot in range(2):
         fill_bias(slot)
-    lax.fori_loop(0, TILES, begin, 0, unroll=4)
+    lax.fori_loop(0, TILES, begin, 0, unroll=2)
 
     scores, weights, fades = (s_even, s_odd), (p_even, p_odd), (f_even, f_odd)
 
@@ -223,29 +214,64 @@
         k, _ = pair(slots)
         scores[b][:, : ROWS * len(slots)] = dot_nt(qx[tile], k)
 
-    def weigh(tile, count, b):
-        s = scores[b][:, : ROWS * count]
+    def weigh(tile, keys, b):
+        s = scores[b][:, :keys]
         before = top[tile]
         high = jnp.maximum(before, jnp.max(s, axis=1, keepdims=True))
-        weights[b][:, : ROWS * count] = jnp.exp2(s - high[:, :1]).astype(jnp.bfloat16)
+        weights[b][:, :keys] = jnp.exp2(s - high[:, :1]).astype(jnp.bfloat16)
         fades[b][...] = jnp.exp2(before - high)
         top[tile] = high
 
-    def gather(tile, slots, b):
-        _, v = pair(slots)
+    def add(tile, v, b):
         fade = fades[b][...]
         acc[tile] = acc[tile] * jnp.concatenate([fade, fade], axis=1) + dot(
-            weights[b][:, : ROWS * len(slots)], jnp.concatenate([v, jnp.ones_like(v)], axis=1)
-        )
+            weights[b][:, : v.shape[0]], jnp.concatenate([v, jnp.ones_like(v)], axis=1)
+        )
+
+    def gather(tile, slots, b):
+        add(tile, pair(slots)[1], b)
+
+    def score_own(tile, b):
+        shard, part = tile // 8, lax.rem(tile, 8)
+        keys = pl.ds(pl.multiple_of(part // 4 * HD, HD), HD)
+        diag = dot_nt(qx[tile, :, :HD], kv[shard, keys, :])
+        scores[b][:, :HD] = jnp.where(lanes <= row + lax.rem(part, 4) * PART, diag, HIDDEN)
+        scores[b][:, HD : HD + 2 * ROWS] = dot_nt(qx[tile], pair([0, 1])[0])
+
+    def gather_own(tile, b):
+        vals = pl.ds(pl.multiple_of(ROWS + lax.rem(tile, 8) // 4 * HD, HD), HD)
+        add(tile, jnp.concatenate([kv[tile // 8, vals, :], pair([0, 1])[1]], axis=0), b)
+
+    def nothing_before():
+        weights[1][...] = jnp.zeros_like(weights[1])
+        fades[1][...] = jnp.ones_like(fades[1])
+
+    def own_turn(turn, carry):
+        for u in range(BAND):
+            tile = turn * BAND + u
+            score_own(jnp.minimum(tile + 1, TILES - 1), (u + 1) % 2)
+            gather_own(jnp.maximum(tile - 1, 0), (u + 1) % 2)
+            weigh(tile, HD + 2 * ROWS, u % 2)
+        return carry
+
+    nothing_before()
+    score_own(0, 0)
+    lax.fori_loop(0, 2, own_turn, 0)
+    gather_own(TILES - 1, 1)
 
     def serve(places, halves=(0, 1)):
         for place in places:
             for half in halves:
                 arrival(2 * place + half).wait_recv()
                 for index, send in enumerate(SENDS):
-                    if send[:2] == (place, half):
+                    if send[:2] == (place, half) and (place > 4 or send[4] not in LATER):
                         kv_copy(index).start()
                 fill_bias(2 * place + half)
+
+    def send_later(half):
+        for index, send in enumerate(SENDS):
+            if 0 < send[0] < 5 and send[1] == half and send[4] in LATER:
+                kv_copy(index).start()
 
     def slots_at(turn):
         step = turn // 2
@@ -279,6 +305,13 @@
                     @pl.when((turn == i) & (c == core))
                     def _():
                         serve(places, ((core + which) % 2,))
+
+        for core in range(2):
+            for i in (1, 2):
+
+                @pl.when((turn == i) & (c == core))
+                def _():
+                    send_later((core + i + 1) % 2)
 
         here = slots_at(turn)
         before = slots_at(jnp.maximum(turn - 1, 0))
@@ -293,11 +326,10 @@
                 gather(tile_at(turn, u - 1), here, other_one)
             else:
                 gather(tile_at(turn + 1, BAND - 1), before, other_one)
-            weigh(tile_at(turn, u), 4, now)
+            weigh(tile_at(turn, u), 4 * ROWS, now)
         return carry
 
-    weights[1][...] = jnp.zeros_like(weights[1])
-    fades[1][...] = jnp.ones_like(fades[1])
+    nothing_before()
     lax.fori_loop(0, 2 * STEPS, early, 0)
     gather(TILES - 1, slots_at(2 * STEPS - 1), 1)
     serve((15,))
@@ -334,14 +366,14 @@
             score(tiles[u + 1] if u < 3 else following, last, (u + 1) % 2)
             if u:
                 gather(tiles[u - 1], last, (u + 1) % 2)
-            weigh(tiles[u], len(last), u % 2)
+            weigh(tiles[u], len(last) * ROWS, u % 2)
         gather(tiles[3], last, 1)
         for tile in tiles:
             both = acc[tile]
             o = (both[:, :HD] / both[:, HD:]).astype(jnp.bfloat16)
             for h in range(GROUP):
                 obuf[tile, :, h * HD : (h + 1) * HD] = o[h * PART : (h + 1) * PART, :]
-        for dx in (1, 2, 3):
+        for dx in (2, 1, 3):
             att_copy(g, dx)[1].start()
 
         @pl.when(lax.rem(g, 2) == 0)
@@ -385,13 +417,6 @@
     lax.fori_loop(0, 4, sent, 0)
     for half in range(2):
         own_copy(half).wait()
-
-
-def update(att_ref, res_ref, gain_ref, stream_ref, normed_ref):
-    stream = res_ref[...] + att_ref[...].astype(jnp.float32)
-    stream_ref[...] = stream
-    inv = lax.rsqrt(jnp.mean(stream * stream, axis=1, keepdims=True) + 1e-05)
-    normed_ref[...] = (stream * inv * gain_ref[...]).astype(jnp.bfloat16)
 
 
 def per_device(queries, keys, values, positions, residual, gain):
@@ -415,10 +440,10 @@
             pltpu.VMEM((TILES, TILE, HD), f32),
             pltpu.VMEM((TILES, TILE, 2 * HD), f32),
             pltpu.VMEM((TILES, PART, GROUP * HD), bf16),
-            pltpu.VMEM((TILE, 6 * ROWS), f32),
-            pltpu.VMEM((TILE, 6 * ROWS), f32),
-            pltpu.VMEM((TILE, 6 * ROWS), bf16),
-            pltpu.VMEM((TILE, 6 * ROWS), bf16),
+            pltpu.VMEM((TILE, 10 * ROWS), f32),
+            pltpu.VMEM((TILE, 10 * ROWS), f32),
+            pltpu.VMEM((TILE, 10 * ROWS), bf16),
+            pltpu.VMEM((TILE, 10 * ROWS), bf16),
             pltpu.VMEM((TILE, HD), f32),
             pltpu.VMEM((TILE, HD), f32),
             dma((5,)),
@@ -435,18 +460,9 @@
             collective_id=0, has_side_effects=True, vmem_limit_bytes=60 * 2**20
         ),
     )(positions.reshape(2, HD), queries, keys, values)
-    block = 16
-    band = pl.BlockSpec((block, width), lambda i: (i, 0))
-    stream, normed = pl.pallas_call(
-        update,
-        grid=(rows // block,),
-        out_shape=(
-            jax.ShapeDtypeStruct((rows, width), f32),
-            jax.ShapeDtypeStruct((rows, width), bf16),
-        ),
-        in_specs=[band, band, pl.BlockSpec((1, width), lambda i: (0, 0))],
-        out_specs=(band, band),
-    )(attended, residual[0], gain.reshape(1, width))
+    stream = residual[0] + attended.astype(f32)
+    inv = lax.rsqrt(jnp.mean(stream * stream, axis=1, keepdims=True) + 1e-05)
+    normed = (stream * inv * gain).astype(bf16)
     return (stream[None], normed[None])
 
 

time: 77.1 us -> 72.8 us (0.944)
  Pallas kernels: 75.4 us -> 67.4 us
  other arithmetic: 0 us -> 3.74 us
    pallas_call x1 -> x0, Pallas kernels: 4.28 us -> none  [per_device(): pl.pallas_call(update, grid=(rows // block,), out_shape=(jax.ShapeDtypeSt...]
    pallas_call x1, Pallas kernels: 71.1 us -> 67.4 us  [per_device(): pl.pallas_call(kernel, out_shape=jax.ShapeDtypeStruct((rows, width), bf16...]
    broadcast_in_dim x0 -> x1, other arithmetic: none -> 2.05 us  [per_device(): return (stream[None], normed[None])]
    reduce_sum x0 -> x1, other arithmetic: none -> 1.68 us  [per_device(): inv = lax.rsqrt(jnp.mean(stream * stream, axis=1, keepdims=True) + 1e-05)]
where the time goes in v2:
time: 72.8 us; the launch traced here: 71.9 us
  Pallas kernels  67.4 us (93%)
  other arithmetic  3.74 us (5%)
    pallas_call x1, Pallas kernels, per_device(): pl.pallas_call(kernel, out_shape=jax.ShapeDtypeStruct((rows, width), bf16...  67.4 us
    broadcast_in_dim x1, other arithmetic, per_device(): return (stream[None], normed[None])  2.05 us
    reduce_sum x1, other arithmetic, per_device(): inv = lax.rsqrt(jnp.mean(stream * stream, axis=1, keepdims=True) + 1e-05)  1.68 us

profile of v2, /device:TPU:0, one launch (start us, length us, event | category | flops | bytes accessed | tf_op | source)
XLA Modules:
  0.0 71.9 jit_solution(16617371385695401964)
XLA Ops:
  0.6 0.0 copy-start.1
  0.6 67.4 %shard_map.77 = bf16[64,8192]{1,0:T(8,128)(2,1)} custom-call(s32[2,128]{1,0:T(2,128)} %bitcast.13, bf16[256,2048]{1,0:T(8,128)(2,1)} %q_hbm.1, bf16[256,256]{1,0:T(8,128)(2,1)} %k_hbm.1, bf16[256,256]{1,0:T(8,128)(2,1)} %v_hbm.1), custom_call_target="tpu_custom_call" | custom-call | tf_op jit(solution)/shard_map/pallas_call | solution.py:429
  68.1 0.0 copy-done.1
  68.1 0.0 copy-start
  68.1 0.0 copy-start.2
  68.1 1.7 %multiply_reduce_fusion = f32[64]{0:T(128)S(1)} fusion(bf16[64,8192]{1,0:T(8,128)(2,1)} %shard_map.77, f32[1,64,8192]{2,1,0:T(8,128)S(1)} %copy-done.1), kind=kLoop, calls=%fused_computation.2 | loop fusion | flops 2097088 | bytes 3145984 | tf_op jit(solution)/shard_map/reduce_sum | solution.py:464
  69.8 0.0 copy-done
  69.8 0.0 copy-done.2
  69.8 2.1 %fusion = (bf16[1,64,8192]{2,1,0:T(8,128)(2,1)}, f32[1,64,8192]{2,1,0:T(8,128)}) fusion(f32[8192]{0:T(1024)S(1)} %copy-done.2, f32[64]{0:T(128)S(1)} %add_rsqrt_fusion, bf16[64,8192]{1,0:T(8,128)(2,1)S(1)} %copy-done, f32[1,64,8192]{2,1,0:T(8,128)S(1)} %copy-done.1), kind=kLoop, calls=%fused_computation.3 | loop fusion | flops 2621440 | bytes 6324480 | tf_op jit(solution)/shard_map/broadcast_in_dim | solution.py:466
  (1 shorter events, 0.0 us)
Async XLA Ops:
  0.6 67.5 %copy-start.1 = (f32[1,64,8192]{2,1,0:T(8,128)S(1)}, f32[1,64,8192]{2,1,0:T(8,128)}, u32[]{:S(2)}) copy-start(f32[1,64,8192]{2,1,0:T(8,128)} %param.10) | copy-start | bytes 6291460
  68.1 1.7 %copy-start = (bf16[64,8192]{1,0:T(8,128)(2,1)S(1)}, bf16[64,8192]{1,0:T(8,128)(2,1)}, u32[]{:S(2)}) copy-start(bf16[64,8192]{1,0:T(8,128)(2,1)} %shard_map.77) | copy-start | bytes 3145732
  68.1 1.7 %copy-start.2 = (f32[8192]{0:T(1024)S(1)}, f32[8192]{0:T(1024)}, u32[]{:S(2)}) copy-start(f32[8192]{0:T(1024)} %param.11) | copy-start | bytes 98308

commit v3 on v2

--- a/solution.py
+++ b/solution.py
@@ -292,26 +292,22 @@
     score(0, slots_at(0), 0)
 
     def early(turn, carry):
-        for i, places, which in SERVED:
-            if which == 2:
-
-                @pl.when(turn == i)
-                def _():
-                    serve(places)
-
-            else:
+        for i in sorted({entry[0] for entry in SERVED} | {1, 2}):
+
+            @pl.when(turn == i)
+            def _():
+                for when, places, which in SERVED:
+                    if when == i and which == 2:
+                        serve(places)
                 for core in range(2):
 
-                    @pl.when((turn == i) & (c == core))
+                    @pl.when(c == core)
                     def _():
-                        serve(places, ((core + which) % 2,))
-
-        for core in range(2):
-            for i in (1, 2):
-
-                @pl.when((turn == i) & (c == core))
-                def _():
-                    send_later((core + i + 1) % 2)
+                        for when, places, which in SERVED:
+                            if when == i and which < 2:
+                                serve(places, ((core + which) % 2,))
+                        if i < 3:
+                            send_later((core + i + 1) % 2)
 
         here = slots_at(turn)
         before = slots_at(jnp.maximum(turn - 1, 0))
@@ -343,11 +339,19 @@
             obuf.at[c * 8 + x * 2 + half], landing(half, 2 * x + c), out_sem.at[half]
         )
 
-    def att_copy(g, dx):
-        half, shard = g // 2, lax.rem(c + 1 + g, 2)
-        there = lax.rem(x + dx, 4)
-        tile = shard * 8 + there * 2 + half
-        return tile, pltpu.make_async_remote_copy(
+    def place_of(g, u):
+        middle = (g == 1) | (g == 2)
+        dx = jnp.where(middle, 1 + 2 * (u // 2), jnp.where(g == 0, 2, 0))
+        return dx, lax.rem(jnp.where(middle, c + g, c + 1 + u // 2), 2), u % 2
+
+    def tile_of(g, u):
+        dx, shard, half = place_of(g, u)
+        return shard * 8 + lax.rem(x + dx, 4) * 2 + half
+
+    def att_copy(g, u):
+        dx, shard, half = place_of(g, u)
+        tile = tile_of(g, u)
+        return pltpu.make_async_remote_copy(
             src_ref=obuf.at[tile],
             dst_ref=landing(half, 2 * x + c),
             send_sem=att_send.at[tile],
@@ -356,39 +360,48 @@
             device_id_type=MESH,
         )
 
-    def finish(g, carry):
-        half, shard = g // 2, lax.rem(c + 1 + g, 2)
-        last = slots_of(LAST)
-        tiles = [shard * 8 + quarter * 2 + half for quarter in range(4)]
-        later = jnp.minimum(g + 1, 3)
-        following = lax.rem(c + 1 + later, 2) * 8 + later // 2
+    def sib_copy(half):
+        tile = sib * 8 + x * 2 + half
+        return pltpu.make_async_remote_copy(
+            src_ref=obuf.at[tile],
+            dst_ref=landing(half, 2 * x + c),
+            send_sem=att_send.at[tile],
+            recv_sem=att_recv.at[half, 2 * x + c],
+            device_id=chip(0, 0, 0, sib),
+            device_id_type=MESH,
+        )
+
+    last = slots_of(LAST)
+
+    def finish(g, more):
         for u in range(4):
-            score(tiles[u + 1] if u < 3 else following, last, (u + 1) % 2)
+            if u < 3:
+                score(tile_of(g, u + 1), last, (u + 1) % 2)
+            elif more:
+                score(tile_of(g + 1, 0), last, 0)
             if u:
-                gather(tiles[u - 1], last, (u + 1) % 2)
-            weigh(tiles[u], len(last) * ROWS, u % 2)
-        gather(tiles[3], last, 1)
-        for tile in tiles:
-            both = acc[tile]
-            o = (both[:, :HD] / both[:, HD:]).astype(jnp.bfloat16)
+                gather(tile_of(g, u - 1), last, (u + 1) % 2)
+            weigh(tile_of(g, u), len(last) * ROWS, u % 2)
+        gather(tile_of(g, 3), last, 1)
+        for u in range(4):
+            tile = tile_of(g, u)
+            total = acc[tile]
+            o = (total[:, :HD] / total[:, HD:]).astype(jnp.bfloat16)
             for h in range(GROUP):
                 obuf[tile, :, h * HD : (h + 1) * HD] = o[h * PART : (h + 1) * PART, :]
-        for dx in (2, 1, 3):
-            att_copy(g, dx)[1].start()
-
-        @pl.when(lax.rem(g, 2) == 0)
-        def _():
-            att_copy(g, 0)[1].start()
-
-        @pl.when(lax.rem(g, 2) == 1)
-        def _():
-            own_copy(half).start()
-
+
+    def finish_and_send(g, carry):
+        finish(g, True)
+        for u in range(4):
+            att_copy(g, u).start()
         return carry
 
-    score(lax.rem(c + 1, 2) * 8, slots_of(LAST), 0)
-    lax.fori_loop(0, 4, finish, 0)
-
+    score(tile_of(0, 0), last, 0)
+    lax.fori_loop(0, 3, finish_and_send, 0)
+    finish(3, False)
+    for half in range(2):
+        sib_copy(half).start()
+        own_copy(half).start()
     for half in range(2):
         for n in range(1, 8):
             source = lax.rem(2 * x + c + n, 8)
@@ -405,16 +418,13 @@
         kv_copy(index).wait_send()
 
     def sent(g, carry):
-        for dx in (1, 2, 3):
-            att_copy(g, dx)[1].wait_send()
-
-        @pl.when(lax.rem(g, 2) == 0)
-        def _():
-            att_copy(g, 0)[1].wait_send()
-
+        for u in range(4):
+            att_copy(g, u).wait_send()
         return carry
 
-    lax.fori_loop(0, 4, sent, 0)
+    lax.fori_loop(0, 3, sent, 0)
+    for half in range(2):
+        sib_copy(half).wait_send()
     for half in range(2):
         own_copy(half).wait()
 

time: 72.8 us -> 70.1 us (0.963)
  Pallas kernels: 67.4 us -> 64.5 us
    pallas_call x1, Pallas kernels: 67.4 us -> 64.5 us  [per_device(): pl.pallas_call(kernel, out_shape=jax.ShapeDtypeStruct((rows, width), bf16...]
where the time goes in v3:
time: 70.1 us; the launch traced here: 68.9 us
  Pallas kernels  64.5 us (92%)
  other arithmetic  3.74 us (5%)
    pallas_call x1, Pallas kernels, per_device(): pl.pallas_call(kernel, out_shape=jax.ShapeDtypeStruct((rows, width), bf16...  64.5 us
    broadcast_in_dim x1, other arithmetic, per_device(): return (stream[None], normed[None])  2.05 us
    reduce_sum x1, other arithmetic, per_device(): inv = lax.rsqrt(jnp.mean(stream * stream, axis=1, keepdims=True) + 1e-05)  1.68 us

profile of v3, /device:TPU:0, one launch (start us, length us, event | category | flops | bytes accessed | tf_op | source)
XLA Modules:
  0.0 68.9 jit_solution(10483343115104180595)
XLA Ops:
  0.6 0.0 copy-start.1
  0.6 64.5 %shard_map.77 = bf16[64,8192]{1,0:T(8,128)(2,1)} custom-call(s32[2,128]{1,0:T(2,128)} %bitcast.13, bf16[256,2048]{1,0:T(8,128)(2,1)} %q_hbm.1, bf16[256,256]{1,0:T(8,128)(2,1)} %k_hbm.1, bf16[256,256]{1,0:T(8,128)(2,1)} %v_hbm.1), custom_call_target="tpu_custom_call" | custom-call | tf_op jit(solution)/shard_map/pallas_call | solution.py:439
  65.1 0.0 copy-done.1
  65.1 0.0 copy-start
  65.2 0.0 copy-start.2
  65.2 1.7 %multiply_reduce_fusion = f32[64]{0:T(128)S(1)} fusion(bf16[64,8192]{1,0:T(8,128)(2,1)} %shard_map.77, f32[1,64,8192]{2,1,0:T(8,128)S(1)} %copy-done.1), kind=kLoop, calls=%fused_computation.2 | loop fusion | flops 2097088 | bytes 3145984 | tf_op jit(solution)/shard_map/reduce_sum | solution.py:474
  66.9 0.0 copy-done
  66.9 0.0 copy-done.2
  66.9 2.1 %fusion = (bf16[1,64,8192]{2,1,0:T(8,128)(2,1)}, f32[1,64,8192]{2,1,0:T(8,128)}) fusion(f32[8192]{0:T(1024)S(1)} %copy-done.2, f32[64]{0:T(128)S(1)} %add_rsqrt_fusion, bf16[64,8192]{1,0:T(8,128)(2,1)S(1)} %copy-done, f32[1,64,8192]{2,1,0:T(8,128)S(1)} %copy-done.1), kind=kLoop, calls=%fused_computation.3 | loop fusion | flops 2621440 | bytes 6324480 | tf_op jit(solution)/shard_map/broadcast_in_dim | solution.py:476
  (1 shorter events, 0.0 us)
Async XLA Ops:
  0.6 64.5 %copy-start.1 = (f32[1,64,8192]{2,1,0:T(8,128)S(1)}, f32[1,64,8192]{2,1,0:T(8,128)}, u32[]{:S(2)}) copy-start(f32[1,64,8192]{2,1,0:T(8,128)} %param.10) | copy-start | bytes 6291460
  65.1 1.7 %copy-start = (bf16[64,8192]{1,0:T(8,128)(2,1)S(1)}, bf16[64,8192]{1,0:T(8,128)(2,1)}, u32[]{:S(2)}) copy-start(bf16[64,8192]{1,0:T(8,128)(2,1)} %shard_map.77) | copy-start | bytes 3145732
  65.2 1.7 %copy-start.2 = (f32[8192]{0:T(1024)S(1)}, f32[8192]{0:T(1024)}, u32[]{:S(2)}) copy-start(f32[8192]{0:T(1024)} %param.11) | copy-start | bytes 98308

commit v4 on v3

--- a/solution.py
+++ b/solution.py
@@ -340,9 +340,9 @@
         )
 
     def place_of(g, u):
-        middle = (g == 1) | (g == 2)
-        dx = jnp.where(middle, 1 + 2 * (u // 2), jnp.where(g == 0, 2, 0))
-        return dx, lax.rem(jnp.where(middle, c + g, c + 1 + u // 2), 2), u % 2
+        middle = g in (1, 2)
+        dx = 1 + 2 * (u // 2) if middle else 2 if g == 0 else 0
+        return dx, lax.rem(c + g if middle else c + 1 + u // 2, 2), u % 2
 
     def tile_of(g, u):
         dx, shard, half = place_of(g, u)
@@ -373,35 +373,32 @@
 
     last = slots_of(LAST)
 
-    def finish(g, more):
-        for u in range(4):
-            if u < 3:
-                score(tile_of(g, u + 1), last, (u + 1) % 2)
-            elif more:
-                score(tile_of(g + 1, 0), last, 0)
-            if u:
-                gather(tile_of(g, u - 1), last, (u + 1) % 2)
-            weigh(tile_of(g, u), len(last) * ROWS, u % 2)
-        gather(tile_of(g, 3), last, 1)
-        for u in range(4):
+    def deliver(g, pair_of):
+        for u in pair_of:
             tile = tile_of(g, u)
             total = acc[tile]
             o = (total[:, :HD] / total[:, HD:]).astype(jnp.bfloat16)
             for h in range(GROUP):
                 obuf[tile, :, h * HD : (h + 1) * HD] = o[h * PART : (h + 1) * PART, :]
-
-    def finish_and_send(g, carry):
-        finish(g, True)
-        for u in range(4):
-            att_copy(g, u).start()
-        return carry
+        for u in pair_of:
+            if g < 3:
+                att_copy(g, u).start()
+            elif u < 2:
+                sib_copy(u).start()
+            else:
+                own_copy(u - 2).start()
 
     score(tile_of(0, 0), last, 0)
-    lax.fori_loop(0, 3, finish_and_send, 0)
-    finish(3, False)
-    for half in range(2):
-        sib_copy(half).start()
-        own_copy(half).start()
+    for i in range(16):
+        if i < 15:
+            score(tile_of((i + 1) // 4, (i + 1) % 4), last, (i + 1) % 2)
+        if i:
+            gather(tile_of((i - 1) // 4, (i - 1) % 4), last, (i + 1) % 2)
+        weigh(tile_of(i // 4, i % 4), len(last) * ROWS, i % 2)
+        if i and i % 2 == 0:
+            deliver((i - 2) // 4, (0, 1) if i % 4 == 2 else (2, 3))
+    gather(tile_of(3, 3), last, 1)
+    deliver(3, (2, 3))
     for half in range(2):
         for n in range(1, 8):
             source = lax.rem(2 * x + c + n, 8)
@@ -417,12 +414,9 @@
     for index in range(len(FIRST), len(SENDS)):
         kv_copy(index).wait_send()
 
-    def sent(g, carry):
+    for g in range(3):
         for u in range(4):
             att_copy(g, u).wait_send()
-        return carry
-
-    lax.fori_loop(0, 3, sent, 0)
     for half in range(2):
         sib_copy(half).wait_send()
     for half in range(2):

time: 70.1 us -> 69 us (0.984)
  no operation moved by 1% of the time
where the time goes in v4:
time: 69 us; the launch traced here: 68.3 us
  Pallas kernels  63.9 us (93%)
  other arithmetic  3.74 us (5%)
  between operations  0.7 us (1%)
    pallas_call x1, Pallas kernels, per_device(): pl.pallas_call(kernel, out_shape=jax.ShapeDtypeStruct((rows, width), bf16...  63.9 us
    broadcast_in_dim x1, other arithmetic, per_device(): return (stream[None], normed[None])  2.05 us
    reduce_sum x1, other arithmetic, per_device(): inv = lax.rsqrt(jnp.mean(stream * stream, axis=1, keepdims=True) + 1e-05)  1.68 us

profile of v4, /device:TPU:0, one launch (start us, length us, event | category | flops | bytes accessed | tf_op | source)
XLA Modules:
  0.0 68.3 jit_solution(15503702359247504014)
XLA Ops:
  0.6 0.0 copy-start.1
  0.6 63.9 %shard_map.77 = bf16[64,8192]{1,0:T(8,128)(2,1)} custom-call(s32[2,128]{1,0:T(2,128)} %bitcast.13, bf16[256,2048]{1,0:T(8,128)(2,1)} %q_hbm.1, bf16[256,256]{1,0:T(8,128)(2,1)} %k_hbm.1, bf16[256,256]{1,0:T(8,128)(2,1)} %v_hbm.1), custom_call_target="tpu_custom_call" | custom-call | tf_op jit(solution)/shard_map/pallas_call | solution.py:433
  64.5 0.0 copy-done.1
  64.5 0.0 copy-start
  64.5 0.0 copy-start.2
  64.6 1.7 %multiply_reduce_fusion = f32[64]{0:T(128)S(1)} fusion(bf16[64,8192]{1,0:T(8,128)(2,1)} %shard_map.77, f32[1,64,8192]{2,1,0:T(8,128)S(1)} %copy-done.1), kind=kLoop, calls=%fused_computation.2 | loop fusion | flops 2097088 | bytes 3145984 | tf_op jit(solution)/shard_map/reduce_sum | solution.py:468
  66.3 0.0 copy-done
  66.3 0.0 copy-done.2
  66.3 2.1 %fusion = (bf16[1,64,8192]{2,1,0:T(8,128)(2,1)}, f32[1,64,8192]{2,1,0:T(8,128)}) fusion(f32[8192]{0:T(1024)S(1)} %copy-done.2, f32[64]{0:T(128)S(1)} %add_rsqrt_fusion, bf16[64,8192]{1,0:T(8,128)(2,1)S(1)} %copy-done, f32[1,64,8192]{2,1,0:T(8,128)S(1)} %copy-done.1), kind=kLoop, calls=%fused_computation.3 | loop fusion | flops 2621440 | bytes 6324480 | tf_op jit(solution)/shard_map/broadcast_in_dim | solution.py:470
  (1 shorter events, 0.0 us)
Async XLA Ops:
  0.6 63.9 %copy-start.1 = (f32[1,64,8192]{2,1,0:T(8,128)S(1)}, f32[1,64,8192]{2,1,0:T(8,128)}, u32[]{:S(2)}) copy-start(f32[1,64,8192]{2,1,0:T(8,128)} %param.10) | copy-start | bytes 6291460
  64.5 1.7 %copy-start = (bf16[64,8192]{1,0:T(8,128)(2,1)S(1)}, bf16[64,8192]{1,0:T(8,128)(2,1)}, u32[]{:S(2)}) copy-start(bf16[64,8192]{1,0:T(8,128)(2,1)} %shard_map.77) | copy-start | bytes 3145732
  64.5 1.7 %copy-start.2 = (f32[8192]{0:T(1024)S(1)}, f32[8192]{0:T(1024)}, u32[]{:S(2)}) copy-start(f32[8192]{0:T(1024)} %param.11) | copy-start | bytes 98308

commit v5 on v4

--- a/solution.py
+++ b/solution.py
@@ -191,8 +191,6 @@
             piece = qraw[shard, rows, h * HD : (h + 1) * HD].astype(jnp.float32) * scale
             qx[tile, h * PART : (h + 1) * PART, :HD] = piece.astype(jnp.bfloat16)
         qx[tile, :, HD:] = jnp.where(lanes == 2 * shard + part // 4, 1.0, 0.0).astype(jnp.bfloat16)
-        top[tile] = jnp.full((TILE, HD), HIDDEN, jnp.float32)
-        acc[tile] = jnp.zeros((TILE, 2 * HD), jnp.float32)
         return carry
 
     def slots_of(places):
@@ -240,7 +238,16 @@
 
     def gather_own(tile, b):
         vals = pl.ds(pl.multiple_of(ROWS + lax.rem(tile, 8) // 4 * HD, HD), HD)
-        add(tile, jnp.concatenate([kv[tile // 8, vals, :], pair([0, 1])[1]], axis=0), b)
+        v = jnp.concatenate([kv[tile // 8, vals, :], pair([0, 1])[1]], axis=0)
+        acc[tile] = dot(
+            weights[b][:, : v.shape[0]], jnp.concatenate([v, jnp.ones_like(v)], axis=1)
+        )
+
+    def weigh_own(tile, keys, b):
+        s = scores[b][:, :keys]
+        high = jnp.broadcast_to(jnp.max(s, axis=1, keepdims=True), (TILE, HD))
+        weights[b][:, :keys] = jnp.exp2(s - high[:, :1]).astype(jnp.bfloat16)
+        top[tile] = high
 
     def nothing_before():
         weights[1][...] = jnp.zeros_like(weights[1])
@@ -251,7 +258,7 @@
             tile = turn * BAND + u
             score_own(jnp.minimum(tile + 1, TILES - 1), (u + 1) % 2)
             gather_own(jnp.maximum(tile - 1, 0), (u + 1) % 2)
-            weigh(tile, HD + 2 * ROWS, u % 2)
+            weigh_own(tile, HD + 2 * ROWS, u % 2)
         return carry
 
     nothing_before()

time: 69 us -> 68.6 us (level)
  no operation moved by 1% of the time
where the time goes in v5:
time: 68.6 us; the launch traced here: 68 us
  Pallas kernels  63.5 us (93%)
  other arithmetic  3.74 us (5%)
  between operations  0.7 us (1%)
    pallas_call x1, Pallas kernels, per_device(): pl.pallas_call(kernel, out_shape=jax.ShapeDtypeStruct((rows, width), bf16...  63.5 us
    broadcast_in_dim x1, other arithmetic, per_device(): return (stream[None], normed[None])  2.05 us
    reduce_sum x1, other arithmetic, per_device(): inv = lax.rsqrt(jnp.mean(stream * stream, axis=1, keepdims=True) + 1e-05)  1.68 us

profile of v5, /device:TPU:0, one launch (start us, length us, event | category | flops | bytes accessed | tf_op | source)
XLA Modules:
  0.0 68.0 jit_solution(12341475625151188209)
XLA Ops:
  0.6 0.0 copy-start.1
  0.6 63.5 %shard_map.77 = bf16[64,8192]{1,0:T(8,128)(2,1)} custom-call(s32[2,128]{1,0:T(2,128)} %bitcast.13, bf16[256,2048]{1,0:T(8,128)(2,1)} %q_hbm.1, bf16[256,256]{1,0:T(8,128)(2,1)} %k_hbm.1, bf16[256,256]{1,0:T(8,128)(2,1)} %v_hbm.1), custom_call_target="tpu_custom_call" | custom-call | tf_op jit(solution)/shard_map/pallas_call | solution.py:440
  64.2 0.0 copy-done.1
  64.2 0.0 copy-start
  64.2 0.0 copy-start.2
  64.2 1.7 %multiply_reduce_fusion = f32[64]{0:T(128)S(1)} fusion(bf16[64,8192]{1,0:T(8,128)(2,1)} %shard_map.77, f32[1,64,8192]{2,1,0:T(8,128)S(1)} %copy-done.1), kind=kLoop, calls=%fused_computation.2 | loop fusion | flops 2097088 | bytes 3145984 | tf_op jit(solution)/shard_map/reduce_sum | solution.py:475
  65.9 0.0 copy-done
  65.9 0.0 copy-done.2
  65.9 2.1 %fusion = (bf16[1,64,8192]{2,1,0:T(8,128)(2,1)}, f32[1,64,8192]{2,1,0:T(8,128)}) fusion(f32[8192]{0:T(1024)S(1)} %copy-done.2, f32[64]{0:T(128)S(1)} %add_rsqrt_fusion, bf16[64,8192]{1,0:T(8,128)(2,1)S(1)} %copy-done, f32[1,64,8192]{2,1,0:T(8,128)S(1)} %copy-done.1), kind=kLoop, calls=%fused_computation.3 | loop fusion | flops 2621440 | bytes 6324480 | tf_op jit(solution)/shard_map/broadcast_in_dim | solution.py:477
  (1 shorter events, 0.0 us)
Async XLA Ops:
  0.6 63.6 %copy-start.1 = (f32[1,64,8192]{2,1,0:T(8,128)S(1)}, f32[1,64,8192]{2,1,0:T(8,128)}, u32[]{:S(2)}) copy-start(f32[1,64,8192]{2,1,0:T(8,128)} %param.10) | copy-start | bytes 6291460
  64.2 1.7 %copy-start = (bf16[64,8192]{1,0:T(8,128)(2,1)S(1)}, bf16[64,8192]{1,0:T(8,128)(2,1)}, u32[]{:S(2)}) copy-start(bf16[64,8192]{1,0:T(8,128)(2,1)} %shard_map.77) | copy-start | bytes 3145732
  64.2 1.7 %copy-start.2 = (f32[8192]{0:T(1024)S(1)}, f32[8192]{0:T(1024)}, u32[]{:S(2)}) copy-start(f32[8192]{0:T(1024)} %param.11) | copy-start | bytes 98308
